TPU v7x, 32 devices: a whole 2x2x4 slice. The times are simulated.
32 devices in a mesh: groups: 2 (over y), row: 4 (over x, core), col: 4 (over z).
Axes of the slice: x: 2, y: 2, z: 4, core: 2. Of those that a mesh axis runs over, the one named last changes fastest.
Arguments:
- head_table: float32 [8192, 256], P(('groups', 'row', 'col')), parts along dimension 0, may hold values from -10 to 10, as said below
- head_accum: float32 [8192], P(('groups', 'row', 'col')), parts along dimension 0, may hold values from 0.1 to 2
- tail_table: float32 [8192, 256], P(('groups', 'row', 'col')), parts along dimension 0, may hold values from -10 to 10, as said below
- tail_accum: float32 [8192], P(('groups', 'row', 'col')), parts along dimension 0, may hold values from 0.1 to 2
- relations: float32 [2048, 256], P('groups'), parts along dimension 0, may hold values from -1.5 to 1.5
- relation_accum: float32 [2048], P('groups'), parts along dimension 0, may hold values from 0.1 to 2
- head_rows: int32 [32, 2, 1024], P(('groups', 'row', 'col')), parts along dimension 0, may hold values from 0 to 255
- tail_rows: int32 [32, 2, 1024], P(('groups', 'row', 'col')), parts along dimension 0, may hold values from 0 to 255
- relation_ids: int32 [32, 2, 1024], P(('groups', 'row', 'col')), parts along dimension 0, may hold values from 0 to 1023
- negative_rows: int32 [32, 2, 256], P(('groups', 'row', 'col')), parts along dimension 0, may hold values from 0 to 255
Outputs:
- head_table_out: float32 [8192, 256], P(('groups', 'row', 'col')), parts along dimension 0
- head_accum_out: float32 [8192], P(('groups', 'row', 'col')), parts along dimension 0
- tail_table_out: float32 [8192, 256], P(('groups', 'row', 'col')), parts along dimension 0
- tail_accum_out: float32 [8192], P(('groups', 'row', 'col')), parts along dimension 0
- relations_out: float32 [2048, 256], P('groups'), parts along dimension 0
- relation_accum_out: float32 [2048], P('groups'), parts along dimension 0
There are 2 independent parts, one for each index of `groups`. A program takes and returns all parts, laid end to end along the dimension named above; each array names one. Nothing has to cross between parts.
Inputs may be any that keep to these rules, and one draw needn't show every extreme that they name: `head_table`: embedding rows of independent entries with row scales that differ. `tail_table`: embedding rows of independent entries with row scales that differ.
All inputs are finite; a program needn't handle non-finite values.
Results may differ from a plain program's by a relative error of at most 0.0003.
Values sent between devices are 32-bit elements; how exact they have to be, the bound alone decides.
A program may use at most 64 MiB of HBM per device.

v0:
```python
import jax
import jax.numpy as jnp
from jax import lax
from jax.sharding import PartitionSpec as P

learn_rate = 0.1


def passed_along(block, axis, distance):
    devices = range(lax.axis_size(axis))
    route = [((i - distance) % len(devices), i) for i in devices]
    return lax.ppermute(block, axis, route)


def rows_onehot(selected, rows_here):
    columns = lax.broadcasted_iota(jnp.int32, (selected.shape[0], rows_here), 1)
    return (selected[:, None] == columns).astype(jnp.float32)


def pick_rows(table, source):
    return jnp.dot(table, source, precision=lax.Precision.HIGHEST)


def add_rows(table, values):
    return jnp.einsum("er,ed->rd", table, values, precision=lax.Precision.HIGHEST)


def edge_terms(head_block, tail_block, relations, head_sel, rel_sel, tail_sel, neg_sel):
    rows_here = head_block.shape[0]
    head_onehot = rows_onehot(head_sel, rows_here)
    tail_onehot = rows_onehot(tail_sel, rows_here)
    neg_onehot = rows_onehot(neg_sel, rows_here)
    rel_onehot = rows_onehot(rel_sel, relations.shape[0])
    heads_e = pick_rows(head_onehot, head_block)
    rels_e = pick_rows(rel_onehot, relations)
    tails_e = pick_rows(tail_onehot, tail_block)
    negatives = pick_rows(neg_onehot, tail_block)
    head_rel = heads_e * rels_e
    positive = jnp.sum(head_rel * tails_e, axis=1)
    scores = jnp.einsum("ed,nd->en", head_rel, negatives, precision=lax.Precision.HIGHEST)
    ceiling = jnp.maximum(positive, jnp.max(scores, axis=1))
    pos_weight = jnp.exp(positive - ceiling)
    neg_weight = jnp.exp(scores - ceiling[:, None])
    denominator = pos_weight + jnp.sum(neg_weight, axis=1)
    pos_grad = pos_weight / denominator - 1.0
    neg_grad = neg_weight / denominator[:, None]
    grad_pair = pos_grad[:, None] * tails_e + jnp.dot(
        neg_grad, negatives, precision=lax.Precision.HIGHEST
    )
    grad_head = add_rows(head_onehot, grad_pair * rels_e)
    grad_rel = add_rows(rel_onehot, grad_pair * heads_e)
    grad_negs = jnp.einsum("en,ed->nd", neg_grad, head_rel, precision=lax.Precision.HIGHEST)
    grad_tail = add_rows(tail_onehot, pos_grad[:, None] * head_rel)
    grad_tail = grad_tail + add_rows(neg_onehot, grad_negs)
    return (grad_head, grad_tail, grad_rel)


def bucket_grads(head_block, tail_block, relations, head_sel, rel_sel, tail_sel, neg_sel):
    edge_total = head_sel.shape[0]
    block_len = min(edge_total, 1024)
    block_count = edge_total // block_len

    def accumulate(block_index, running):
        terms = edge_terms(head_block, tail_block, relations, head_sel, rel_sel, tail_sel, neg_sel)
        return (running[0] + terms[0], running[1] + terms[1], running[2] + terms[2])

    start_sums = (
        jnp.zeros(head_block.shape, jnp.float32),
        jnp.zeros(tail_block.shape, jnp.float32),
        jnp.zeros(relations.shape, jnp.float32),
    )
    return lax.fori_loop(0, block_count, accumulate, start_sums)


def adagrad_rows(weights, accumulator, gradient):
    updated = accumulator + jnp.mean(gradient * gradient, axis=1)
    return (weights - learn_rate * gradient / jnp.sqrt(updated)[:, None], updated)


def shards(
    head_table,
    head_accum,
    tail_table,
    tail_accum,
    relations,
    relation_accum,
    head_rows,
    tail_rows,
    relation_ids,
    negative_rows,
):
    grad_head, grad_tail, rel_one = bucket_grads(
        head_table,
        tail_table,
        relations,
        head_rows[0, 0],
        relation_ids[0, 0],
        tail_rows[0, 0],
        negative_rows[0, 0],
    )
    head_new, head_acc_new = adagrad_rows(head_table, head_accum, grad_head)
    tail_new, tail_acc_new = adagrad_rows(tail_table, tail_accum, grad_tail)
    head_moved, head_acc_moved = passed_along((head_new, head_acc_new), "row", 1)
    tail_moved, tail_acc_moved = passed_along((tail_new, tail_acc_new), "col", 1)
    grad_head, grad_tail, rel_two = bucket_grads(
        head_moved,
        tail_moved,
        relations,
        head_rows[0, 1],
        relation_ids[0, 1],
        tail_rows[0, 1],
        negative_rows[0, 1],
    )
    head_final, head_acc_final = adagrad_rows(head_moved, head_acc_moved, grad_head)
    tail_final, tail_acc_final = adagrad_rows(tail_moved, tail_acc_moved, grad_tail)
    rel_total = lax.psum(rel_one + rel_two, ("row", "col"))
    relations_new, rel_acc_new = adagrad_rows(relations, relation_accum, rel_total)
    return (head_final, head_acc_final, tail_final, tail_acc_final, relations_new, rel_acc_new)


def solution(mesh):
    return jax.shard_map(
        shards,
        mesh=mesh,
        in_specs=(
            P(("groups", "row", "col"), None),
            P(("groups", "row", "col")),
            P(("groups", "row", "col"), None),
            P(("groups", "row", "col")),
            P("groups", None),
            P("groups"),
            P(("groups", "row", "col"), None, None),
            P(("groups", "row", "col"), None, None),
            P(("groups", "row", "col"), None, None),
            P(("groups", "row", "col"), None, None),
        ),
        out_specs=(
            P(("groups", "row", "col"), None),
            P(("groups", "row", "col")),
            P(("groups", "row", "col"), None),
            P(("groups", "row", "col")),
            P("groups", None),
            P("groups"),
        ),
        check_vma=False,
    )
```

profile of v0, /device:TPU:1, one launch (start us, length us, event | category | flops | bytes accessed | tf_op | source)
XLA Modules:
  0.0 149.5 jit_solution(16982798232294543471)
XLA Ops:
  10.3 1.3 fusion.51
  11.6 3.6 %fusion.3 = f32[1024,256]{0,1:T(8,128)S(1)} fusion(f32[1024,256]{1,0:T(8,128)} %param.14, s32[1024]{0:T(1024)S(1)} %bitcast.40), kind=kOutput, calls=%fused_computation.5 | convolution fusion | flops 3222274048 | bytes 2101248 | tf_op jit(solution)/shard_map/while/body/eval_jaxpr/dot_general | solution.py:21
  16.2 1.0 multiply_reduce_fusion.2
  17.1 1.1 fusion.67
  18.4 1.2 fusion.47
  20.9 2.2 %collective-permute-start.3 = (f32[256]{0:T(256)S(1)}, f32[256]{0:T(256)S(1)}, u32[]{:S(2)}, u32[]{:S(2)}) collective-permute-start(f32[256]{0:T(256)S(1)} %get-tuple-element.76), channel_id=1, source_target_pairs={{3,0},{0,1},{1,2},{2,3},{7,4},{4,5},{5,6},{6,7},{11,8},{8,9},{9,10... | collective-permute-start | bytes 3080 | tf_op jit(solution)/shard_map/ppermute | solution.py:12
  23.1 1.3 convolution_add_fusion
  24.4 0.8 multiply_reduce_fusion.6
  25.4 2.1 %collective-permute-start.2 = (f32[256]{0:T(256)S(1)}, f32[256]{0:T(256)S(1)}, u32[]{:S(2)}, u32[]{:S(2)}) collective-permute-start(f32[256]{0:T(256)S(1)} %get-tuple-element.89), channel_id=1, source_target_pairs={{12,0},{0,4},{4,8},{8,12},{13,1},{1,5},{5,9},{9,13},{14,2},{2,6},{... | collective-permute-start | bytes 3080 | tf_op jit(solution)/shard_map/ppermute | solution.py:12
  27.7 1.4 collective-permute-start.1
  29.8 3.8 %fusion.4 = f32[1024,256]{1,0:T(8,128)S(1)} fusion(s32[1024]{0:T(1024)S(1)} %bitcast.41, f32[1024,256]{0,1:T(8,128)} %copy-done.4, f32[1024,256]{0,1:T(8,128)S(1)} %fusion.28), kind=kOutput, calls=%fused_computation.6 | convolution fusion | flops 3223584768 | bytes 3149824 | tf_op jit(solution)/shard_map/while/body/eval_jaxpr/er,ed->rd/dot_general | solution.py:25
  33.6 2.3 %fusion.1 = f32[1024,256]{0,1:T(8,128)S(1)} fusion(f32[1024,256]{1,0:T(8,128)S(1)} %copy-done.3, s32[1024]{0:T(1024)S(1)} %bitcast.34), kind=kOutput, calls=%fused_computation.2 | convolution fusion | flops 3222274048 | bytes 2101248 | tf_op jit(solution)/shard_map/while/body/eval_jaxpr/dot_general | solution.py:21
  35.9 1.0 collective-permute-done.1
  38.0 0.9 multiply_reduce_fusion.1
  39.0 1.1 fusion.68
  40.3 1.1 fusion.43
  41.4 1.2 fusion.45
  43.5 1.2 multiply_reduce_fusion.4
  44.7 3.7 %fusion.12 = f32[1024,256]{1,0:T(8,128)} fusion(f32[1024,256]{1,0:T(8,128)S(1)} %fusion.4, s32[1024]{0:T(1024)S(1)} %bitcast.35, f32[1024,256]{0,1:T(8,128)S(1)} %fusion.24, f32[1024,256]{0,1:T(8,128)S(1)} %fusion.45, f32[1024,256]{0,1:T(8,128)S(1)} %get-tuple-element.111, f32[1024]{0:T(1024)S(1)} %get-tuple-element.92), kind=kOutput, calls=%fused_computation.12 | convolution fusion | flops 3224371200 | bytes 5251072 | tf_op jit(solution)/shard_map/while/body/eval_jaxpr/er,ed->rd/dot_general | solution.py:25
  49.5 0.8 copy.20
  50.9 0.8 copy.21
  51.8 87.5 %all-reduce.2.cloned.1.call-done = f32[1024,256]{1,0:T(8,128)} async-done(((f32[1024,256]{1,0:T(8,128)}), f32[1024,256]{1,0:T(8,128)}) %all-reduce.2.cloned.1.call-update) | async-done | bytes 1048592 | tf_op jit(solution)/shard_map/psum | solution.py:116
  139.3 1.5 %multiply_reduce_fusion = f32[1024]{0:T(1024)S(1)} fusion(f32[1024,256]{1,0:T(8,128)} %all-reduce.2.cloned.1.call-done), kind=kLoop, calls=%fused_computation.17 | loop fusion | flops 523264 | bytes 1052672 | tf_op jit(solution)/shard_map/reduce_sum | solution.py:76
  141.4 1.2 divide_subtract_fusion
  (50 shorter events, 10.9 us)
Async XLA Ops:
  7.2 132.1 %all-reduce.2.cloned.1.call-start = ((), (), s32[]{:S(2)}) async-start(), calls=%async_computation | async-start | bytes 2097152 | tf_op jit(solution)/shard_map/psum | solution.py:116
  11.6 3.6 %copy-start.2 = (f32[256,256]{1,0:T(8,128)S(1)}, f32[256,256]{1,0:T(8,128)}, u32[]{:S(2)}) copy-start(f32[256,256]{1,0:T(8,128)} %param.10) | copy-start | bytes 786436
  15.2 1.0 copy-start.1
  19.6 1.3 copy-start.6
  20.9 29.4 %collective-permute-start.3 = (f32[256]{0:T(256)S(1)}, f32[256]{0:T(256)S(1)}, u32[]{:S(2)}, u32[]{:S(2)}) collective-permute-start(f32[256]{0:T(256)S(1)} %get-tuple-element.76), channel_id=1, source_target_pairs={{3,0},{0,1},{1,2},{2,3},{7,4},{4,5},{5,6},{6,7},{11,8},{8,9},{9,10... | collective-permute-start | bytes 3080 | tf_op jit(solution)/shard_map/ppermute | solution.py:12
  24.4 1.0 copy-start.4
  24.4 1.0 copy-start.7
  25.4 23.5 %collective-permute-start.2 = (f32[256]{0:T(256)S(1)}, f32[256]{0:T(256)S(1)}, u32[]{:S(2)}, u32[]{:S(2)}) collective-permute-start(f32[256]{0:T(256)S(1)} %get-tuple-element.89), channel_id=1, source_target_pairs={{12,0},{0,4},{4,8},{8,12},{13,1},{1,5},{5,9},{9,13},{14,2},{2,6},{... | collective-permute-start | bytes 3080 | tf_op jit(solution)/shard_map/ppermute | solution.py:12
  27.7 9.3 %collective-permute-start.1 = (f32[256,256]{0,1:T(8,128)S(1)}, f32[256,256]{0,1:T(8,128)S(1)}, u32[]{:S(2)}, u32[]{:S(2)}) collective-permute-start(f32[256,256]{0,1:T(8,128)S(1)} %divide_subtract_fusion.3), channel_id=1, source_target_pairs={{3,0},{0,1},{1,2},{2,3},{7,4},{4,5},{5,6},{6,7},{11,8},{8,9},{9,10... | collective-permute-start | bytes 786440 | tf_op jit(solution)/shard_map/ppermute | solution.py:12
  29.2 4.4 %copy-start.3 = (f32[1024,256]{1,0:T(8,128)S(1)}, f32[1024,256]{1,0:T(8,128)}, u32[]{:S(2)}) copy-start(f32[1024,256]{1,0:T(8,128)} %param.14) | copy-start | bytes 3145732
  29.2 8.1 %collective-permute-start = (f32[256,256]{0,1:T(8,128)S(1)}, f32[256,256]{0,1:T(8,128)S(1)}, u32[]{:S(2)}, u32[]{:S(2)}) collective-permute-start(f32[256,256]{0,1:T(8,128)S(1)} %divide_subtract_fusion.4), channel_id=1, source_target_pairs={{12,0},{0,4},{4,8},{8,12},{13,1},{1,5},{5,9},{9,13},{14,2},{2,6},{... | collective-permute-start | bytes 786440 | tf_op jit(solution)/shard_map/ppermute | solution.py:12
  50.9 89.9 %copy-start.5 = (f32[1024]{0:T(1024)S(1)}, f32[1024]{0:T(1024)}, u32[]{:S(2)}) copy-start(f32[1024]{0:T(1024)} %param.15) | copy-start | bytes 12292
  139.3 2.1 %copy-start = (f32[1024,256]{1,0:T(8,128)S(1)}, f32[1024,256]{1,0:T(8,128)}, u32[]{:S(2)}) copy-start(f32[1024,256]{1,0:T(8,128)} %all-reduce.2.cloned.1.call-done) | copy-start | bytes 3145732
Sparse Core Ops, SparseCore 0:
  48.5 90.6 all-reduce.1
where the time goes:
time: 151 us; the launch traced here: 149 us
  waiting for transfers between devices  88.5 us (59%)
  matrix products  30.1 us (20%)
  between operations  14.4 us (10%)
  starting transfers between devices  6.18 us (4%)
  local copies, waits for them, and re-layouts  5.31 us (4%)
  other arithmetic  5 us (3%)
    psum x1, waiting for transfers between devices, shards(): rel_total = lax.psum(rel_one + rel_two, ('row', 'col'))  87.5 us
    dot_general x8, matrix products, add_rows(): jnp.einsum('er,ed->rd', table, values, precision=lax.Precision.HIGHEST)  12.1 us
    dot_general x8, matrix products, pick_rows(): return jnp.dot(table, source, precision=lax.Precision.HIGHEST)  10.9 us
    ppermute x4, starting transfers between devices, passed_along(): return lax.ppermute(block, axis, route)  6.14 us
  transfers between devices with their start and end apart: 5, of which 2 were waited for; matrix products, arithmetic and copies ran while one was open for 16% of the time, Pallas kernels for 0%

commit v1 on v0

v1 whole, which is shorter than its diff:
```python
import functools

import jax
import jax.numpy as jnp
from jax import lax
from jax.experimental import pallas as pl
from jax.experimental.pallas import tpu as pltpu
from jax.sharding import PartitionSpec as P

learn_rate = 0.1
edge_tile = 256
f32 = jnp.float32
bf16 = jnp.bfloat16
MESH = pl.DeviceIdType.MESH


def split(value):
    high = value.astype(bf16)
    return high, (value - high.astype(f32)).astype(bf16)


def dot(a, b):
    return jnp.dot(a, b, preferred_element_type=f32)


def dot_nt(a, b):
    return lax.dot_general(a, b, (((1,), (1,)), ((), ())), preferred_element_type=f32)


def onehot(ids, count):
    rows = lax.broadcasted_iota(jnp.int32, (count, ids.shape[1]), 0)
    return rows == ids


def column(row):
    wide = jnp.broadcast_to(row, (128, row.shape[1]))
    return jnp.transpose(wide)[:, :1]


def as_row(col):
    wide = jnp.broadcast_to(col, (col.shape[0], 128))
    return jnp.transpose(wide)[:8]


def adagrad(weights, accum_row, gradient):
    width = gradient.shape[1]
    mean = jnp.sum(gradient * gradient, axis=1, keepdims=True) * (1.0 / width)
    updated = column(accum_row) + mean
    return weights - gradient * (learn_rate / jnp.sqrt(updated)), as_row(updated)


def kernel(
    n_row,
    n_col,
    head_ref,
    head_acc_ref,
    tail_ref,
    tail_acc_ref,
    rel_ref,
    rel_acc_ref,
    head_ids,
    tail_ids,
    rel_ids,
    neg_ids,
    head_out,
    head_acc_out,
    tail_out,
    tail_acc_out,
    rel_out,
    rel_acc_out,
    rel_t,
    rel_hot,
    rels_e,
    heads_e,
    hq_hi,
    hq_lo,
    wt_hi,
    wt_lo,
    by_head_hi,
    by_head_lo,
    by_rel_hi,
    by_rel_lo,
    head_send,
    tail_send,
    head_in,
    tail_in,
    grad,
    core_in,
    x_in,
    z_in,
    total,
    move_send,
    move_recv,
    core_send,
    core_recv,
    xs_send,
    xs_recv,
    zs_send,
    zs_recv,
    zg_send,
    zg_recv,
    xg_send,
    xg_recv,
    cg_send,
    cg_recv,
):
    n_x = n_row // 2
    rows, width = head_ref.shape
    n_rel = rel_ref.shape[0]
    edges = head_ids.shape[1]
    half = width // 2
    x_rows = n_rel // n_x
    z_rows = x_rows // n_col
    r = lax.axis_index("row")
    c = lax.axis_index("col")
    x = lax.div(r, 2)
    h = lax.rem(r, 2)
    sibling = x * 2 + (1 - h)

    barrier = pltpu.get_barrier_semaphore()
    for k in range(1, n_row):
        pl.semaphore_signal(barrier, inc=1, device_id={"row": lax.rem(r + k, n_row)}, device_id_type=MESH)
    for k in range(1, n_col):
        pl.semaphore_signal(barrier, inc=1, device_id={"col": lax.rem(c + k, n_col)}, device_id_type=MESH)

    def remote(src, dst, send, recv, device):
        return pltpu.make_async_remote_copy(
            src_ref=src, dst_ref=dst, send_sem=send, recv_sem=recv, device_id=device, device_id_type=MESH
        )

    def gather_rels(b):
        for e0 in range(0, edges, edge_tile):
            cols = slice(e0, e0 + edge_tile)
            hot = onehot(rel_ids[b : b + 1, cols], n_rel).astype(bf16)
            rel_hot[b, :, cols] = hot
            both = dot(rel_t[...], hot)
            rels_e[b, :, cols] = both[:width] + both[width:]

    def weigh(b, head, tail):
        head_t = jnp.concatenate(split(jnp.transpose(head)), axis=0)
        tail_hi, tail_lo = split(tail)
        tail_both = jnp.concatenate([tail_hi, tail_lo], axis=0)
        counts = jnp.sum(onehot(neg_ids[b : b + 1, :], rows).astype(f32), axis=1, keepdims=True)
        for e0 in range(0, edges, edge_tile):
            cols = slice(e0, e0 + edge_tile)
            both = dot(head_t, onehot(head_ids[b : b + 1, cols], rows).astype(bf16))
            heads = both[:rows] + both[rows:]
            heads_e[:, cols] = heads
            hi, lo = split(heads * rels_e[b, :, cols])
            hq_hi[:, cols] = hi
            hq_lo[:, cols] = lo
            both = dot(tail_both, hi)
            scores = both[:rows] + both[rows:] + dot(tail_hi, lo)
            tail_hot = onehot(tail_ids[b : b + 1, cols], rows)
            positive = jnp.sum(jnp.where(tail_hot, scores, 0.0), axis=0, keepdims=True)
            scores = jnp.where(counts > 0.0, scores, -3e38)
            ceiling = jnp.maximum(jnp.max(scores, axis=0, keepdims=True), positive)
            pos_exp = jnp.exp(positive - ceiling)
            neg_exp = jnp.exp(scores - ceiling) * counts
            inverse = 1.0 / (pos_exp + jnp.sum(neg_exp, axis=0, keepdims=True))
            weight = neg_exp * inverse + jnp.where(tail_hot, pos_exp * inverse - 1.0, 0.0)
            hi, lo = split(weight)
            wt_hi[:, cols] = hi
            wt_lo[:, cols] = lo

    def tail_gradient():
        return dot_nt(wt_hi[...], hq_hi[...]) + dot_nt(wt_hi[...], hq_lo[...]) + dot_nt(wt_lo[...], hq_hi[...])

    def pair_gradients(b, tail):
        tail_t_hi, tail_t_lo = split(jnp.transpose(tail))
        tail_t = jnp.concatenate([tail_t_hi, tail_t_lo], axis=0)
        for e0 in range(0, edges, edge_tile):
            cols = slice(e0, e0 + edge_tile)
            both = dot(tail_t, wt_hi[:, cols])
            pair = both[:width] + both[width:] + dot(tail_t_hi, wt_lo[:, cols])
            hi, lo = split(pair * rels_e[b, :, cols])
            by_head_hi[:, cols] = hi
            by_head_lo[:, cols] = lo
            hi, lo = split(pair * heads_e[:, cols])
            by_rel_hi[:, cols] = hi
            by_rel_lo[:, cols] = lo

    def head_gradient(b):
        hot = onehot(head_ids[b : b + 1, :], rows).astype(bf16)
        return dot_nt(hot, by_head_hi[...]) + dot_nt(hot, by_head_lo[...])

    rel_t[...] = jnp.concatenate(split(jnp.transpose(rel_ref[...])), axis=0)
    gather_rels(0)
    weigh(0, head_ref[...], tail_ref[...])
    tail_new, tail_acc_new = adagrad(tail_ref[...], tail_acc_ref[...], tail_gradient())
    tail_send[:rows] = tail_new
    tail_send[rows:] = tail_acc_new
    pl.semaphore_wait(barrier, n_row + n_col - 2)
    tail_move = remote(tail_send, tail_in, move_send.at[0], move_recv.at[0], {"col": lax.rem(c + 1, n_col)})
    tail_move.start()
    pair_gradients(0, tail_ref[...])
    head_new, head_acc_new = adagrad(head_ref[...], head_acc_ref[...], head_gradient(0))
    head_send[:rows] = head_new
    head_send[rows:] = head_acc_new
    head_move = remote(head_send, head_in, move_send.at[1], move_recv.at[1], {"row": lax.rem(r + 1, n_row)})
    head_move.start()
    rel_one = dot_nt(rel_hot[0], by_rel_hi[...]) + dot_nt(rel_hot[0], by_rel_lo[...])
    grad[0] = rel_one[:, :half]
    grad[1] = rel_one[:, half:]
    gather_rels(1)
    head_move.wait()
    tail_move.wait()

    weigh(1, head_in[:rows], tail_in[:rows])
    pair_gradients(1, tail_in[:rows])

    def x_start(i):
        return pl.multiple_of(lax.rem(x + i, n_x) * x_rows, x_rows)

    def z_start(i, k):
        return pl.multiple_of((lax.rem(x + i, n_x) * n_col + lax.rem(c + k, n_col)) * z_rows, z_rows)

    x_order = list(range(1, n_x)) + [0]
    z_order = list(range(1, n_col)) + [0]
    core_moves = {}
    for i in x_order:
        here = pl.ds(x_start(i), x_rows)
        part = dot_nt(rel_hot[1, here], by_rel_hi[...]) + dot_nt(rel_hot[1, here], by_rel_lo[...])
        grad[0, here] = grad[0, here] + part[:, :half]
        grad[1, here] = grad[1, here] + part[:, half:]
        core_moves[i] = remote(
            grad.at[1 - h, here], core_in.at[here], core_send.at[i], core_recv.at[i], {"row": sibling}
        )
        core_moves[i].start()

    x_moves = {}
    for i in x_order:
        core_moves[i].wait_recv()
        for k in z_order:
            here = pl.ds(z_start(i, k), z_rows)
            grad[h, here] = grad[h, here] + core_in[here]
            if i:
                slot = (i - 1) * n_col + k
                x_moves[i, k] = remote(
                    grad.at[h, here],
                    x_in.at[slot],
                    xs_send.at[slot],
                    xs_recv.at[slot],
                    {"row": lax.rem(x + i, n_x) * 2 + h},
                )
                x_moves[i, k].start()

    head_final, head_acc_final = adagrad(head_in[:rows], head_in[rows : rows + 1], head_gradient(1))
    head_out[...] = head_final
    head_acc_out[...] = head_acc_final[:1]
    tail_final, tail_acc_final = adagrad(tail_in[:rows], tail_in[rows : rows + 1], tail_gradient())
    tail_out[...] = tail_final
    tail_acc_out[...] = tail_acc_final[:1]

    z_moves = {}
    for k in z_order:
        here = pl.ds(z_start(0, k), z_rows)
        value = grad[h, here]
        for i in range(1, n_x):
            x_moves[i, k].wait_recv()
            value = value + x_in[(i - 1) * n_col + k]
        grad[h, here] = value
        if k:
            z_moves[k] = remote(
                grad.at[h, here],
                z_in.at[k - 1],
                zs_send.at[k - 1],
                zs_recv.at[k - 1],
                {"col": lax.rem(c + k, n_col)},
            )
            z_moves[k].start()

    mine = pl.ds(z_start(0, 0), z_rows)
    value = grad[h, mine]
    for k in range(1, n_col):
        z_moves[k].wait_recv()
        value = value + z_in[k - 1]
    total[h, mine] = value

    gathers = []

    def spread(slot_x, slot_z, to_x):
        piece = total.at[h, pl.ds(z_start(slot_x, slot_z), z_rows)]
        if to_x:
            for i in range(1, n_x):
                slot = (i - 1) * n_col + slot_z
                gathers.append(
                    remote(piece, piece, xg_send.at[slot], xg_recv.at[slot], {"row": lax.rem(x + i, n_x) * 2 + h})
                )
                gathers[-1].start()
        slot = slot_x * n_col + slot_z
        gathers.append(remote(piece, piece, cg_send.at[slot], cg_recv.at[slot], {"row": sibling}))
        gathers[-1].start()

    piece = total.at[h, mine]
    for k in range(1, n_col):
        gathers.append(
            remote(piece, piece, zg_send.at[k - 1], zg_recv.at[k - 1], {"col": lax.rem(c + k, n_col)})
        )
        gathers[-1].start()
    spread(0, 0, True)

    def arrived(piece, sem):
        pltpu.make_async_copy(piece, piece, sem).wait()

    for k in range(1, n_col):
        from_z = n_col - k
        arrived(total.at[h, pl.ds(z_start(0, from_z), z_rows)], zg_recv.at[k - 1])
        spread(0, from_z, True)
    for k in [0] + list(range(n_col - 1, 0, -1)):
        for i in range(1, n_x):
            from_x = n_x - i
            arrived(total.at[h, pl.ds(z_start(from_x, k), z_rows)], xg_recv.at[(i - 1) * n_col + k])
            spread(from_x, k, False)
    for i in range(n_x):
        for k in range(n_col):
            arrived(total.at[1 - h, pl.ds(z_start(i, k), z_rows)], cg_recv.at[i * n_col + k])

    for r0 in range(0, n_rel, rows):
        here = slice(r0, r0 + rows)
        both = jnp.concatenate([total[0, here], total[1, here]], axis=1)
        rel_new, rel_acc_new = adagrad(rel_ref[here], rel_acc_ref[:, here], both)
        rel_out[here] = rel_new
        rel_acc_out[:, here] = rel_acc_new[:1]

    for move in list(core_moves.values()) + list(x_moves.values()) + list(z_moves.values()) + gathers:
        move.wait_send()


def shards(
    n_row,
    n_col,
    head_table,
    head_accum,
    tail_table,
    tail_accum,
    relations,
    relation_accum,
    head_rows,
    tail_rows,
    relation_ids,
    negative_rows,
):
    rows, width = head_table.shape
    n_rel = relations.shape[0]
    buckets, edges = head_rows.shape[1:]
    n_x = n_row // 2
    half = width // 2
    z_rows = n_rel // (n_x * n_col)
    shape = jax.ShapeDtypeStruct
    vmem = pl.BlockSpec(memory_space=pltpu.VMEM)
    dma = pltpu.SemaphoreType.DMA
    x_slots = max(1, (n_x - 1) * n_col)
    z_slots = max(1, n_col - 1)
    edge_piece = pltpu.VMEM((width, edges), bf16)
    moved = pltpu.VMEM((rows + 8, width), f32)
    outs = pl.pallas_call(
        functools.partial(kernel, n_row, n_col),
        out_shape=(
            shape((rows, width), f32),
            shape((1, rows), f32),
            shape((rows, width), f32),
            shape((1, rows), f32),
            shape((n_rel, width), f32),
            shape((1, n_rel), f32),
        ),
        in_specs=[vmem] * 10,
        out_specs=(vmem,) * 6,
        scratch_shapes=[
            pltpu.VMEM((2 * width, n_rel), bf16),
            pltpu.VMEM((buckets, n_rel, edges), bf16),
            pltpu.VMEM((buckets, width, edges), f32),
            pltpu.VMEM((width, edges), f32),
            edge_piece,
            edge_piece,
            pltpu.VMEM((rows, edges), bf16),
            pltpu.VMEM((rows, edges), bf16),
            edge_piece,
            edge_piece,
            edge_piece,
            edge_piece,
            moved,
            moved,
            moved,
            moved,
            pltpu.VMEM((2, n_rel, half), f32),
            pltpu.VMEM((n_rel, half), f32),
            pltpu.VMEM((x_slots, z_rows, half), f32),
            pltpu.VMEM((z_slots, z_rows, half), f32),
            pltpu.VMEM((2, n_rel, half), f32),
            dma((2,)),
            dma((2,)),
            dma((n_x,)),
            dma((n_x,)),
            dma((x_slots,)),
            dma((x_slots,)),
            dma((z_slots,)),
            dma((z_slots,)),
            dma((z_slots,)),
            dma((z_slots,)),
            dma((x_slots,)),
            dma((x_slots,)),
            dma((n_x * n_col,)),
            dma((n_x * n_col,)),
        ],
        compiler_params=pltpu.CompilerParams(
            collective_id=0, has_side_effects=True, vmem_limit_bytes=50 * 2**20
        ),
    )(
        head_table,
        head_accum.reshape(1, rows),
        tail_table,
        tail_accum.reshape(1, rows),
        relations,
        relation_accum.reshape(1, n_rel),
        head_rows[0],
        tail_rows[0],
        relation_ids[0],
        negative_rows[0],
    )
    return (outs[0], outs[1][0], outs[2], outs[3][0], outs[4], outs[5][0])


def solution(mesh):
    block = P(("groups", "row", "col"))
    return jax.shard_map(
        functools.partial(shards, mesh.shape["row"], mesh.shape["col"]),
        mesh=mesh,
        in_specs=(block, block, block, block, P("groups"), P("groups"), block, block, block, block),
        out_specs=(block, block, block, block, P("groups"), P("groups")),
        check_vma=False,
    )
```

time: 151 us -> 54.2 us (0.36)
  waiting for transfers between devices: 88.5 us -> 0 us
  Pallas kernels: 0 us -> 42.5 us
  matrix products: 30.1 us -> 0 us
  between operations: 14.4 us -> 0.68 us
  starting transfers between devices: 6.18 us -> 0 us
  local copies, waits for them, and re-layouts: 5.31 us -> 10.7 us
  other arithmetic: 5 us -> 0 us
    psum x1 -> x0, waiting for transfers between devices: 87.5 us -> none  [shards(): rel_total = lax.psum(rel_one + rel_two, ('row', 'col'))]
    pallas_call x0 -> x1, Pallas kernels: none -> 42.5 us  [shards(): pl.pallas_call(functools.partial(kernel, n_row, n_col), out_shape=(shape(...]
    dot_general x22 -> x0, matrix products: 30.1 us -> none  [the longest x8 12.1 us: add_rows(): jnp.einsum('er,ed->rd', table, values, precision=lax.Precision.HIGHEST)]
    unnamed x20 -> x26, local copies, waits for them, and re-layouts: 2.2 us -> 10.7 us
    ppermute x4 -> x0, starting transfers between devices: 6.14 us -> none  [passed_along(): return lax.ppermute(block, axis, route)]
    slice x4 -> x0, local copies, waits for them, and re-layouts: 3.11 us -> none  [the longest x1 0.78 us: shards(): tail_rows[0, 1]]
    reduce_sum x3 -> x0, other arithmetic: 1.87 us -> none  [the longest x1 1.52 us: adagrad_rows(): updated = accumulator + jnp.mean(gradient * gradient, axis=1)]
    sqrt x5 -> x0, other arithmetic: 1.74 us -> none  [adagrad_rows(): jnp.sqrt(updated)[:, None]]
  transfers between devices with their start and end apart: 5 -> 0, of which waited for: 2 -> 0; matrix products, arithmetic and copies ran while one was open for 16% -> 0% of each run, Pallas kernels for 0% -> 0%
where the time goes in v1:
time: 54.2 us; the launch traced here: 53.8 us
  Pallas kernels  42.5 us (78%)
  local copies, waits for them, and re-layouts  10.7 us (20%)
  between operations  0.68 us (1%)
    pallas_call x1, Pallas kernels, shards(): pl.pallas_call(functools.partial(kernel, n_row, n_col), out_shape=(shape(...  42.5 us
    unnamed x26, local copies, waits for them, and re-layouts  10.7 us

profile of v1, /device:TPU:1, one launch (start us, length us, event | category | flops | bytes accessed | tf_op | source)
XLA Modules:
  0.0 53.8 jit_solution(49689016533294485)
XLA Ops:
  0.6 0.0 copy-start.3
  0.6 0.0 copy-start.6
  0.7 0.0 copy-start.8
  0.7 0.7 %copy-done.3 = s32[1,2,1024]{2,1,0:T(2,128)S(1)} copy-done((s32[1,2,1024]{2,1,0:T(2,128)S(1)}, s32[1,2,1024]{2,1,0:T(2,128)}, u32[]{:S(2)}) %copy-start.3) | copy-done | bytes 8216
  1.3 0.0 copy-done.6
  1.3 0.0 copy-done.8
  1.3 0.0 copy-start
  1.3 1.2 %copy-done = f32[1024,256]{1,0:T(8,128)S(1)} copy-done((f32[1024,256]{1,0:T(8,128)S(1)}, f32[1024,256]{1,0:T(8,128)}, u32[]{:S(2)}) %copy-start) | copy-done | bytes 1048600
  2.6 0.0 copy-start.1
  2.6 0.9 %copy-done.1 = f32[256,256]{1,0:T(8,128)S(1)} copy-done((f32[256,256]{1,0:T(8,128)S(1)}, f32[256,256]{1,0:T(8,128)}, u32[]{:S(2)}) %copy-start.1) | copy-done | bytes 262168
  3.5 0.0 copy-start.2
  3.5 0.9 %copy-done.2 = f32[256,256]{1,0:T(8,128)S(1)} copy-done((f32[256,256]{1,0:T(8,128)S(1)}, f32[256,256]{1,0:T(8,128)}, u32[]{:S(2)}) %copy-start.2) | copy-done | bytes 262168
  4.5 0.7 %copy-done.4 = s32[1,2,1024]{2,1,0:T(2,128)S(1)} copy-done((s32[1,2,1024]{2,1,0:T(2,128)S(1)}, s32[1,2,1024]{2,1,0:T(2,128)}, u32[]{:S(2)}) %copy-start.4) | copy-done | bytes 8216
  5.2 0.0 copy-start.5
  5.2 0.7 %copy-done.5 = s32[1,2,1024]{2,1,0:T(2,128)S(1)} copy-done((s32[1,2,1024]{2,1,0:T(2,128)S(1)}, s32[1,2,1024]{2,1,0:T(2,128)}, u32[]{:S(2)}) %copy-start.5) | copy-done | bytes 8216
  5.9 0.7 %copy-done.7 = s32[1,2,256]{2,1,0:T(2,128)S(1)} copy-done((s32[1,2,256]{2,1,0:T(2,128)S(1)}, s32[1,2,256]{2,1,0:T(2,128)}, u32[]{:S(2)}) %copy-start.7) | copy-done | bytes 2072
  6.6 0.7 %copy-done.9 = f32[256]{0:T(256)S(1)} copy-done((f32[256]{0:T(256)S(1)}, f32[256]{0:T(256)}, u32[]{:S(2)}) %copy-start.9) | copy-done | bytes 1048
  7.2 42.5 %shard_map.145 = (f32[256,256]{1,0:T(8,128)S(1)}, f32[1,256]{1,0:T(1,128)S(1)}, f32[256,256]{1,0:T(8,128)S(1)}, f32[1,256]{1,0:T(1,128)S(1)}, f32[1024,256]{1,0:T(8,128)S(1)}, /*index=5*/f32[1,1024]{1,0:T(1,128)S(1)}) custom-call(f32[256,256]{1,0:T(8,128)S(1)} %copy-done.1, f32[1,256]{1,0:T(1,128)S(1)} %bitcast.16, f32[256,256]{1,0:T(8,128)S(1)} %copy-done.2, ...), custom_call_target="tpu_custom_call" | custom-call | tf_op jit(solution)/shard_map/pallas_call | solution.py:357
  49.7 0.7 %copy.22 = f32[256,256]{1,0:T(8,128)} copy(f32[256,256]{1,0:T(8,128)S(1)} %get-tuple-element.24) | data formatting | bytes 524288
  50.4 0.6 %copy.23 = f32[256]{0:T(256)} copy(f32[256]{0:T(256)S(1)} %bitcast.19) | data formatting | bytes 2048
  51.0 0.7 %copy.24 = f32[256,256]{1,0:T(8,128)} copy(f32[256,256]{1,0:T(8,128)S(1)} %get-tuple-element.26) | data formatting | bytes 524288
  51.7 0.6 %copy.25 = f32[256]{0:T(256)} copy(f32[256]{0:T(256)S(1)} %bitcast.18) | data formatting | bytes 2048
  52.3 1.0 %copy.26 = f32[1024,256]{1,0:T(8,128)} copy(f32[1024,256]{1,0:T(8,128)S(1)} %get-tuple-element.28) | data formatting | bytes 2097152
  53.2 0.6 %copy.27 = f32[1024]{0:T(1024)} copy(f32[1024]{0:T(1024)S(1)} %bitcast.14) | data formatting | bytes 8192
  (3 shorter events, 0.0 us)
Async XLA Ops:
  0.6 0.7 %copy-start.3 = (s32[1,2,1024]{2,1,0:T(2,128)S(1)}, s32[1,2,1024]{2,1,0:T(2,128)}, u32[]{:S(2)}) copy-start(s32[1,2,1024]{2,1,0:T(2,128)} %param.16) | copy-start | bytes 24580
  0.6 0.7 %copy-start.6 = (f32[1024]{0:T(1024)S(1)}, f32[1024]{0:T(1024)}, u32[]{:S(2)}) copy-start(f32[1024]{0:T(1024)} %param.15) | copy-start | bytes 12292
  0.7 0.7 %copy-start.8 = (f32[256]{0:T(256)S(1)}, f32[256]{0:T(256)}, u32[]{:S(2)}) copy-start(f32[256]{0:T(256)} %param.11) | copy-start | bytes 3076
  1.3 1.2 %copy-start = (f32[1024,256]{1,0:T(8,128)S(1)}, f32[1024,256]{1,0:T(8,128)}, u32[]{:S(2)}) copy-start(f32[1024,256]{1,0:T(8,128)} %rel_ref.1) | copy-start | bytes 3145732
  2.6 0.9 %copy-start.1 = (f32[256,256]{1,0:T(8,128)S(1)}, f32[256,256]{1,0:T(8,128)}, u32[]{:S(2)}) copy-start(f32[256,256]{1,0:T(8,128)} %head_ref.1) | copy-start | bytes 786436
  3.5 0.9 %copy-start.2 = (f32[256,256]{1,0:T(8,128)S(1)}, f32[256,256]{1,0:T(8,128)}, u32[]{:S(2)}) copy-start(f32[256,256]{1,0:T(8,128)} %tail_ref.1) | copy-start | bytes 786436
  4.5 0.7 %copy-start.4 = (s32[1,2,1024]{2,1,0:T(2,128)S(1)}, s32[1,2,1024]{2,1,0:T(2,128)}, u32[]{:S(2)}) copy-start(s32[1,2,1024]{2,1,0:T(2,128)} %param.17) | copy-start | bytes 24580
  5.2 0.7 %copy-start.5 = (s32[1,2,1024]{2,1,0:T(2,128)S(1)}, s32[1,2,1024]{2,1,0:T(2,128)}, u32[]{:S(2)}) copy-start(s32[1,2,1024]{2,1,0:T(2,128)} %param.18) | copy-start | bytes 24580
  5.9 0.7 %copy-start.7 = (s32[1,2,256]{2,1,0:T(2,128)S(1)}, s32[1,2,256]{2,1,0:T(2,128)}, u32[]{:S(2)}) copy-start(s32[1,2,256]{2,1,0:T(2,128)} %param.19) | copy-start | bytes 6148
  6.6 0.7 %copy-start.9 = (f32[256]{0:T(256)S(1)}, f32[256]{0:T(256)}, u32[]{:S(2)}) copy-start(f32[256]{0:T(256)} %param.13) | copy-start | bytes 3076

commit v2 on v1

--- a/solution.py
+++ b/solution.py
@@ -52,6 +52,22 @@
 def kernel(
     n_row,
     n_col,
+    head_hbm,
+    head_acc_hbm,
+    tail_hbm,
+    tail_acc_hbm,
+    rel_hbm,
+    rel_acc_hbm,
+    head_ids_hbm,
+    tail_ids_hbm,
+    rel_ids_hbm,
+    neg_ids_hbm,
+    head_out_hbm,
+    head_acc_out_hbm,
+    tail_out_hbm,
+    tail_acc_out_hbm,
+    rel_out_hbm,
+    rel_acc_out_hbm,
     head_ref,
     head_acc_ref,
     tail_ref,
@@ -62,12 +78,16 @@
     tail_ids,
     rel_ids,
     neg_ids,
+    load_sems,
     head_out,
     head_acc_out,
     tail_out,
     tail_acc_out,
     rel_out,
     rel_acc_out,
+    rel_acc_wide,
+    store_sems,
+    rel_store_sems,
     rel_t,
     rel_hot,
     rels_e,
@@ -117,6 +137,22 @@
     h = lax.rem(r, 2)
     sibling = x * 2 + (1 - h)
 
+    pairs = (
+        (rel_hbm, rel_ref),
+        (rel_ids_hbm, rel_ids),
+        (head_hbm, head_ref),
+        (head_ids_hbm, head_ids),
+        (tail_hbm, tail_ref),
+        (tail_ids_hbm, tail_ids),
+        (neg_ids_hbm, neg_ids),
+        (tail_acc_hbm, tail_acc_ref),
+        (head_acc_hbm, head_acc_ref),
+        (rel_acc_hbm, rel_acc_ref),
+    )
+    loads = [pltpu.make_async_copy(src, dst, load_sems.at[n]) for n, (src, dst) in enumerate(pairs)]
+    for load in loads:
+        load.start()
+
     barrier = pltpu.get_barrier_semaphore()
     for k in range(1, n_row):
         pl.semaphore_signal(barrier, inc=1, device_id={"row": lax.rem(r + k, n_row)}, device_id_type=MESH)
@@ -184,8 +220,12 @@
         hot = onehot(head_ids[b : b + 1, :], rows).astype(bf16)
         return dot_nt(hot, by_head_hi[...]) + dot_nt(hot, by_head_lo[...])
 
+    loads[0].wait()
     rel_t[...] = jnp.concatenate(split(jnp.transpose(rel_ref[...])), axis=0)
+    loads[1].wait()
     gather_rels(0)
+    for load in loads[2:]:
+        load.wait()
     weigh(0, head_ref[...], tail_ref[...])
     tail_new, tail_acc_new = adagrad(tail_ref[...], tail_acc_ref[...], tail_gradient())
     tail_send[:rows] = tail_new
@@ -209,6 +249,12 @@
     weigh(1, head_in[:rows], tail_in[:rows])
     pair_gradients(1, tail_in[:rows])
 
+    stores = []
+
+    def keep(src, dst, sem):
+        stores.append(pltpu.make_async_copy(src, dst, sem))
+        stores[-1].start()
+
     def x_start(i):
         return pl.multiple_of(lax.rem(x + i, n_x) * x_rows, x_rows)
 
@@ -248,9 +294,16 @@
     head_final, head_acc_final = adagrad(head_in[:rows], head_in[rows : rows + 1], head_gradient(1))
     head_out[...] = head_final
     head_acc_out[...] = head_acc_final[:1]
+    keep(head_out, head_out_hbm, store_sems.at[0])
+    keep(head_acc_out, head_acc_out_hbm, store_sems.at[1])
     tail_final, tail_acc_final = adagrad(tail_in[:rows], tail_in[rows : rows + 1], tail_gradient())
     tail_out[...] = tail_final
     tail_acc_out[...] = tail_acc_final[:1]
+    keep(tail_out, tail_out_hbm, store_sems.at[2])
+    keep(tail_acc_out, tail_acc_out_hbm, store_sems.at[3])
+    for r0 in range(0, n_rel, 128):
+        wide = jnp.broadcast_to(rel_acc_ref[:, r0 : r0 + 128], (128, 128))
+        rel_acc_wide[r0 : r0 + 128] = jnp.transpose(wide)
 
     z_moves = {}
     for k in z_order:
@@ -307,24 +360,55 @@
         from_z = n_col - k
         arrived(total.at[h, pl.ds(z_start(0, from_z), z_rows)], zg_recv.at[k - 1])
         spread(0, from_z, True)
-    for k in [0] + list(range(n_col - 1, 0, -1)):
+    def finish(i, k):
+        here = pl.ds(z_start(i, k), z_rows)
+        arrived(total.at[1 - h, here], cg_recv.at[i * n_col + k])
+        both = jnp.concatenate([total[0, here], total[1, here]], axis=1)
+        mean = jnp.sum(both * both, axis=1, keepdims=True) * (1.0 / width)
+        updated = rel_acc_wide[here] + mean
+        rel_acc_wide[here] = updated
+        rel_out[here] = rel_ref[here] - both * (learn_rate / jnp.sqrt(updated))[:, :1]
+        keep(rel_out.at[here], rel_out_hbm.at[here], rel_store_sems.at[i * n_col + k])
+
+    arrivals = [0] + list(range(n_col - 1, 0, -1))
+    for k in arrivals:
         for i in range(1, n_x):
             from_x = n_x - i
             arrived(total.at[h, pl.ds(z_start(from_x, k), z_rows)], xg_recv.at[(i - 1) * n_col + k])
             spread(from_x, k, False)
-    for i in range(n_x):
-        for k in range(n_col):
-            arrived(total.at[1 - h, pl.ds(z_start(i, k), z_rows)], cg_recv.at[i * n_col + k])
-
-    for r0 in range(0, n_rel, rows):
-        here = slice(r0, r0 + rows)
-        both = jnp.concatenate([total[0, here], total[1, here]], axis=1)
-        rel_new, rel_acc_new = adagrad(rel_ref[here], rel_acc_ref[:, here], both)
-        rel_out[here] = rel_new
-        rel_acc_out[:, here] = rel_acc_new[:1]
-
+        finish(0, k)
+    for k in arrivals:
+        for i in range(1, n_x):
+            finish(n_x - i, k)
+    for r0 in range(0, n_rel, 128):
+        rel_acc_out[:, r0 : r0 + 128] = jnp.transpose(rel_acc_wide[r0 : r0 + 128])[:1]
+    keep(rel_acc_out, rel_acc_out_hbm, store_sems.at[4])
+    for move in stores:
+        move.wait()
     for move in list(core_moves.values()) + list(x_moves.values()) + list(z_moves.values()) + gathers:
         move.wait_send()
+
+
+def store(*refs):
+    ins, outs, held = refs[:6], refs[6:12], refs[12:18]
+    load_sems, store_sems = refs[18:]
+    tiles = [(n, pl.ds(q, 128)) for n in (4, 0, 2) for q in range(0, ins[n].shape[0], 128)]
+    tiles += [(n, slice(None)) for n in (5, 1, 3)]
+    loads = [
+        pltpu.make_async_copy(ins[n].at[part], held[n].at[part], load_sems.at[i])
+        for i, (n, part) in enumerate(tiles)
+    ]
+    stores = [
+        pltpu.make_async_copy(held[n].at[part], outs[n].at[part], store_sems.at[i])
+        for i, (n, part) in enumerate(tiles)
+    ]
+    for load in loads:
+        load.start()
+    for load, move in zip(loads, stores):
+        load.wait()
+        move.start()
+    for move in stores:
+        move.wait()
 
 
 def shards(
@@ -348,7 +432,6 @@
     half = width // 2
     z_rows = n_rel // (n_x * n_col)
     shape = jax.ShapeDtypeStruct
-    vmem = pl.BlockSpec(memory_space=pltpu.VMEM)
     dma = pltpu.SemaphoreType.DMA
     x_slots = max(1, (n_x - 1) * n_col)
     z_slots = max(1, n_col - 1)
@@ -364,9 +447,29 @@
             shape((n_rel, width), f32),
             shape((1, n_rel), f32),
         ),
-        in_specs=[vmem] * 10,
-        out_specs=(vmem,) * 6,
+        in_specs=[pl.BlockSpec(memory_space=pltpu.HBM)] * 10,
+        out_specs=(pl.BlockSpec(memory_space=pltpu.HBM),) * 6,
         scratch_shapes=[
+            pltpu.VMEM((rows, width), f32),
+            pltpu.VMEM((1, rows), f32),
+            pltpu.VMEM((rows, width), f32),
+            pltpu.VMEM((1, rows), f32),
+            pltpu.VMEM((n_rel, width), f32),
+            pltpu.VMEM((1, n_rel), f32),
+            pltpu.VMEM((buckets, edges), jnp.int32),
+            pltpu.VMEM((buckets, edges), jnp.int32),
+            pltpu.VMEM((buckets, edges), jnp.int32),
+            pltpu.VMEM(negative_rows.shape[1:], jnp.int32),
+            dma((10,)),
+            pltpu.VMEM((rows, width), f32),
+            pltpu.VMEM((1, rows), f32),
+            pltpu.VMEM((rows, width), f32),
+            pltpu.VMEM((1, rows), f32),
+            pltpu.VMEM((n_rel, width), f32),
+            pltpu.VMEM((1, n_rel), f32),
+            pltpu.VMEM((n_rel, 128), f32),
+            dma((5,)),
+            dma((n_x * n_col,)),
             pltpu.VMEM((2 * width, n_rel), bf16),
             pltpu.VMEM((buckets, n_rel, edges), bf16),
             pltpu.VMEM((buckets, width, edges), f32),
@@ -404,7 +507,7 @@
             dma((n_x * n_col,)),
         ],
         compiler_params=pltpu.CompilerParams(
-            collective_id=0, has_side_effects=True, vmem_limit_bytes=50 * 2**20
+            collective_id=0, has_side_effects=True, vmem_limit_bytes=62 * 2**20
         ),
     )(
         head_table,
@@ -418,6 +521,15 @@
         relation_ids[0],
         negative_rows[0],
     )
+    outs = pl.pallas_call(
+        store,
+        out_shape=tuple(shape(out.shape, f32) for out in outs),
+        in_specs=[pl.BlockSpec(memory_space=pltpu.HBM)] * 6,
+        out_specs=(pl.BlockSpec(memory_space=pltpu.HBM),) * 6,
+        scratch_shapes=[pltpu.VMEM(out.shape, f32) for out in outs]
+        + [dma(((n_rel + 2 * rows) // 128 + 3,)), dma(((n_rel + 2 * rows) // 128 + 3,))],
+        compiler_params=pltpu.CompilerParams(vmem_limit_bytes=62 * 2**20),
+    )(*outs)
     return (outs[0], outs[1][0], outs[2], outs[3][0], outs[4], outs[5][0])
 
 

time: 54.2 us -> 47.3 us (0.87)
  local copies, waits for them, and re-layouts: 10.7 us -> 0 us
  Pallas kernels: 42.5 us -> 46.4 us
    unnamed x26 -> x0, local copies, waits for them, and re-layouts: 10.7 us -> none
    pallas_call x0 -> x1, Pallas kernels: none -> 2.39 us  [shards(): pl.pallas_call(store, out_shape=tuple((shape(out.shape, f32) for out in o...]
    pallas_call x1, Pallas kernels: 42.5 us -> 44.1 us  [shards(): pl.pallas_call(functools.partial(kernel, n_row, n_col), out_shape=(shape(...]
where the time goes in v2:
time: 47.3 us; the launch traced here: 47.1 us
  Pallas kernels  46.4 us (98%)
  between operations  0.64 us (1%)
    pallas_call x1, Pallas kernels, shards(): pl.pallas_call(functools.partial(kernel, n_row, n_col), out_shape=(shape(...  44.1 us
    pallas_call x1, Pallas kernels, shards(): pl.pallas_call(store, out_shape=tuple((shape(out.shape, f32) for out in o...  2.39 us

profile of v2, /device:TPU:1, one launch (start us, length us, event | category | flops | bytes accessed | tf_op | source)
XLA Modules:
  0.0 47.1 jit_solution(10201106094944691292)
XLA Ops:
  0.6 44.1 %shard_map.145 = (f32[256,256]{1,0:T(8,128)}, f32[1,256]{1,0:T(1,128)}, f32[256,256]{1,0:T(8,128)}, f32[1,256]{1,0:T(1,128)}, f32[1024,256]{1,0:T(8,128)}, /*index=5*/f32[1,1024]{1,0:T(1,128)}) custom-call(f32[256,256]{1,0:T(8,128)} %head_hbm.1, f32[1,256]{1,0:T(1,128)} %bitcast.15, f32[256,256]{1,0:T(8,128)} %tail_hbm.1, f32[1,256]{1,0:T(1,128)} %bitcast.16, ...), custom_call_target="tpu_custom_call" | custom-call | tf_op jit(solution)/shard_map/pallas_call | solution.py:440
  44.7 2.4 %shard_map.146 = (f32[256,256]{1,0:T(8,128)}, f32[1,256]{1,0:T(1,128)}, f32[256,256]{1,0:T(8,128)}, f32[1,256]{1,0:T(1,128)}, f32[1024,256]{1,0:T(8,128)}, /*index=5*/f32[1,1024]{1,0:T(1,128)}) custom-call(f32[256,256]{1,0:T(8,128)} %get-tuple-element.18.refs_0_, f32[1,256]{1,0:T(1,128)} %get-tuple-element.19.refs_1_, f32[256,256]{1,0:T(8,128)} %get-tuple-element.20.refs_2_, ...), custom_call_target="tpu_custom_call" | custom-call | tf_op jit(solution)/shard_map/pallas_call | solution.py:524

commit v3 on v2

--- a/solution.py
+++ b/solution.py
@@ -172,11 +172,8 @@
             both = dot(rel_t[...], hot)
             rels_e[b, :, cols] = both[:width] + both[width:]
 
-    def weigh(b, head, tail):
+    def project(b, head):
         head_t = jnp.concatenate(split(jnp.transpose(head)), axis=0)
-        tail_hi, tail_lo = split(tail)
-        tail_both = jnp.concatenate([tail_hi, tail_lo], axis=0)
-        counts = jnp.sum(onehot(neg_ids[b : b + 1, :], rows).astype(f32), axis=1, keepdims=True)
         for e0 in range(0, edges, edge_tile):
             cols = slice(e0, e0 + edge_tile)
             both = dot(head_t, onehot(head_ids[b : b + 1, cols], rows).astype(bf16))
@@ -185,7 +182,15 @@
             hi, lo = split(heads * rels_e[b, :, cols])
             hq_hi[:, cols] = hi
             hq_lo[:, cols] = lo
-            both = dot(tail_both, hi)
+
+    def weigh(b, tail):
+        tail_hi, tail_lo = split(tail)
+        tail_both = jnp.concatenate([tail_hi, tail_lo], axis=0)
+        counts = jnp.sum(onehot(neg_ids[b : b + 1, :], rows).astype(f32), axis=1, keepdims=True)
+        for e0 in range(0, edges, edge_tile):
+            cols = slice(e0, e0 + edge_tile)
+            lo = hq_lo[:, cols]
+            both = dot(tail_both, hq_hi[:, cols])
             scores = both[:rows] + both[rows:] + dot(tail_hi, lo)
             tail_hot = onehot(tail_ids[b : b + 1, cols], rows)
             positive = jnp.sum(jnp.where(tail_hot, scores, 0.0), axis=0, keepdims=True)
@@ -200,7 +205,8 @@
             wt_lo[:, cols] = lo
 
     def tail_gradient():
-        return dot_nt(wt_hi[...], hq_hi[...]) + dot_nt(wt_hi[...], hq_lo[...]) + dot_nt(wt_lo[...], hq_hi[...])
+        hi = wt_hi[...]
+        return dot_nt(hi, hq_hi[...]) + dot_nt(hi, hq_lo[...]) + dot_nt(wt_lo[...], hq_hi[...])
 
     def pair_gradients(b, tail):
         tail_t_hi, tail_t_lo = split(jnp.transpose(tail))
@@ -216,6 +222,11 @@
             by_rel_hi[:, cols] = hi
             by_rel_lo[:, cols] = lo
 
+    def pass_on(sent, held, slot, device):
+        move = remote(sent, held, move_send.at[slot], move_recv.at[slot], device)
+        move.start()
+        return move
+
     def head_gradient(b):
         hot = onehot(head_ids[b : b + 1, :], rows).astype(bf16)
         return dot_nt(hot, by_head_hi[...]) + dot_nt(hot, by_head_lo[...])
@@ -226,27 +237,26 @@
     gather_rels(0)
     for load in loads[2:]:
         load.wait()
-    weigh(0, head_ref[...], tail_ref[...])
+    project(0, head_ref[...])
+    weigh(0, tail_ref[...])
     tail_new, tail_acc_new = adagrad(tail_ref[...], tail_acc_ref[...], tail_gradient())
     tail_send[:rows] = tail_new
     tail_send[rows:] = tail_acc_new
     pl.semaphore_wait(barrier, n_row + n_col - 2)
-    tail_move = remote(tail_send, tail_in, move_send.at[0], move_recv.at[0], {"col": lax.rem(c + 1, n_col)})
-    tail_move.start()
+    tail_move = pass_on(tail_send, tail_in, 0, {"col": lax.rem(c + 1, n_col)})
     pair_gradients(0, tail_ref[...])
     head_new, head_acc_new = adagrad(head_ref[...], head_acc_ref[...], head_gradient(0))
     head_send[:rows] = head_new
     head_send[rows:] = head_acc_new
-    head_move = remote(head_send, head_in, move_send.at[1], move_recv.at[1], {"row": lax.rem(r + 1, n_row)})
-    head_move.start()
+    head_move = pass_on(head_send, head_in, 1, {"row": lax.rem(r + 1, n_row)})
     rel_one = dot_nt(rel_hot[0], by_rel_hi[...]) + dot_nt(rel_hot[0], by_rel_lo[...])
     grad[0] = rel_one[:, :half]
     grad[1] = rel_one[:, half:]
     gather_rels(1)
     head_move.wait()
+    project(1, head_in[:rows])
     tail_move.wait()
-
-    weigh(1, head_in[:rows], tail_in[:rows])
+    weigh(1, tail_in[:rows])
     pair_gradients(1, tail_in[:rows])
 
     stores = []

time: 47.3 us -> 46.7 us (0.987)
  Pallas kernels: 46.4 us -> 45.9 us
    pallas_call x1, Pallas kernels: 44.1 us -> 43.5 us  [shards(): pl.pallas_call(functools.partial(kernel, n_row, n_col), out_shape=(shape(...]
where the time goes in v3:
time: 46.7 us; the launch traced here: 46.5 us
  Pallas kernels  45.9 us (98%)
  between operations  0.64 us (1%)
    pallas_call x1, Pallas kernels, shards(): pl.pallas_call(functools.partial(kernel, n_row, n_col), out_shape=(shape(...  43.5 us
    pallas_call x1, Pallas kernels, shards(): pl.pallas_call(store, out_shape=tuple((shape(out.shape, f32) for out in o...  2.39 us

profile of v3, /device:TPU:1, one launch (start us, length us, event | category | flops | bytes accessed | tf_op | source)
XLA Modules:
  0.0 46.5 jit_solution(11700960106112992333)
XLA Ops:
  0.6 43.5 %shard_map.145 = (f32[256,256]{1,0:T(8,128)}, f32[1,256]{1,0:T(1,128)}, f32[256,256]{1,0:T(8,128)}, f32[1,256]{1,0:T(1,128)}, f32[1024,256]{1,0:T(8,128)}, /*index=5*/f32[1,1024]{1,0:T(1,128)}) custom-call(f32[256,256]{1,0:T(8,128)} %head_hbm.1, f32[1,256]{1,0:T(1,128)} %bitcast.15, f32[256,256]{1,0:T(8,128)} %tail_hbm.1, f32[1,256]{1,0:T(1,128)} %bitcast.16, ...), custom_call_target="tpu_custom_call" | custom-call | tf_op jit(solution)/shard_map/pallas_call | solution.py:450
  44.2 2.4 %shard_map.146 = (f32[256,256]{1,0:T(8,128)}, f32[1,256]{1,0:T(1,128)}, f32[256,256]{1,0:T(8,128)}, f32[1,256]{1,0:T(1,128)}, f32[1024,256]{1,0:T(8,128)}, /*index=5*/f32[1,1024]{1,0:T(1,128)}) custom-call(f32[256,256]{1,0:T(8,128)} %get-tuple-element.18.refs_0_, f32[1,256]{1,0:T(1,128)} %get-tuple-element.19.refs_1_, f32[256,256]{1,0:T(8,128)} %get-tuple-element.20.refs_2_, ...), custom_call_target="tpu_custom_call" | custom-call | tf_op jit(solution)/shard_map/pallas_call | solution.py:534
